TPU v7x, 128 devices: a whole 4x4x4 slice. The times are simulated.
128 devices in a mesh: seq: 32 (over y, z, core), ch: 4 (over x).
Axes of the slice: x: 4, y: 4, z: 4, core: 2. Of those that a mesh axis runs over, the one named last changes fastest.
Arguments:
- gate_in: bfloat16 [8192, 4096], P('seq', 'ch'), may hold values from -80 to 80
- key_in: bfloat16 [8192, 4096], P('seq', 'ch'), may hold values from -6 to 6
- value_in: bfloat16 [8192, 4096], P('seq', 'ch'), may hold values from -6 to 6
- long_filter: bfloat16 [8192, 4096], P('seq', 'ch'), may hold values from -2 to 2
- gate_short: float32 [3, 4096], P(None, 'ch'), may hold values from -3 to 3
- key_short: float32 [3, 4096], P(None, 'ch'), may hold values from -3 to 3
- value_short: float32 [3, 4096], P(None, 'ch'), may hold values from -3 to 3
- skip_gain: float32 [4096], P('ch'), may hold values from 0.5 to 1.5
- norm_gain: float32 [4096], P('ch'), may hold values from 0.5 to 1.5
Outputs:
- mixed: bfloat16 [8192, 4096], P('seq', 'ch')
All inputs are finite; a program needn't handle non-finite values.
Results may differ from a plain program's by a relative error of at most 0.0057.
Values may be sent and summed in bfloat16 or wider, within the bound.
A program may use at most 64 MiB of HBM per device.

v0:
```python
import math

import jax
import jax.numpy as jnp
from jax import lax
from jax.sharding import PartitionSpec as P

FACT = 128


exact = lax.Precision.HIGH


def passed_along(array, axis, by):
    size = lax.axis_size(axis)
    pairs = [(i, i + by) for i in range(size) if 0 <= i + by < size]
    return lax.ppermute(array, axis, pairs)


def short_conv(rows, prev, taps):
    full = jnp.concatenate([prev, rows], axis=0).astype(jnp.float32)
    return taps[0] * full[2:] + taps[1] * full[1:-1] + taps[2] * full[:-2]


def dft_table(length, sign):
    steps = jnp.arange(length, dtype=jnp.int32)
    angle = (
        sign
        * 2.0
        * math.pi
        * (steps[:, None] * steps[None, :] % length).astype(jnp.float32)
        / length
    )
    return (jnp.cos(angle), jnp.sin(angle))


def twiddle_table(first, second, sign):
    total = first * second
    rows = jnp.arange(first, dtype=jnp.int32)[:, None]
    cols = jnp.arange(second, dtype=jnp.int32)[None, :]
    angle = sign * 2.0 * math.pi * (rows * cols % total).astype(jnp.float32) / total
    return (jnp.cos(angle), jnp.sin(angle))


def forward(real_part, factor):
    lanes, half, second = real_part.shape
    first_re, first_im = dft_table(factor, -1.0)
    first_re = first_re[:, :half]
    first_im = first_im[:, :half]
    step_re = jnp.einsum("ka,cab->ckb", first_re, real_part, precision=exact)
    step_im = jnp.einsum("ka,cab->ckb", first_im, real_part, precision=exact)
    twist_re, twist_im = twiddle_table(factor, second, -1.0)
    turned_re = step_re * twist_re - step_im * twist_im
    turned_im = step_re * twist_im + step_im * twist_re
    last_re, last_im = dft_table(second, -1.0)
    spec_re = jnp.einsum("ckb,bm->ckm", turned_re, last_re, precision=exact) - jnp.einsum(
        "ckb,bm->ckm", turned_im, last_im, precision=exact
    )
    spec_im = jnp.einsum("ckb,bm->ckm", turned_re, last_im, precision=exact) + jnp.einsum(
        "ckb,bm->ckm", turned_im, last_re, precision=exact
    )
    return (spec_re, spec_im)


def inverse(prod_re, prod_im, factor):
    lanes, first, second = prod_re.shape
    last_re, last_im = dft_table(second, 1.0)
    step_re = jnp.einsum("ckm,mn->ckn", prod_re, last_re, precision=exact) - jnp.einsum(
        "ckm,mn->ckn", prod_im, last_im, precision=exact
    )
    step_im = jnp.einsum("ckm,mn->ckn", prod_re, last_im, precision=exact) + jnp.einsum(
        "ckm,mn->ckn", prod_im, last_re, precision=exact
    )
    twist_re, twist_im = twiddle_table(factor, second, 1.0)
    turned_re = step_re * twist_re - step_im * twist_im
    turned_im = step_re * twist_im + step_im * twist_re
    first_re, first_im = dft_table(factor, 1.0)
    half = factor // 2
    output = jnp.einsum("pk,ckn->cpn", first_re[:half], turned_re, precision=exact) - jnp.einsum(
        "pk,ckn->cpn", first_im[:half], turned_im, precision=exact
    )
    return output / (factor * second)


def long_conv(product, taps, skip_part):
    length, lanes = product.shape
    factor = FACT
    second = 2 * length // factor
    signal = product.astype(jnp.float32).T.reshape(lanes, factor // 2, second)
    kernel = taps.astype(jnp.float32).T.reshape(lanes, factor // 2, second)
    signal_re, signal_im = forward(signal, factor)
    kernel_re, kernel_im = forward(kernel, factor)
    prod_re = signal_re * kernel_re - signal_im * kernel_im
    prod_im = signal_re * kernel_im + signal_im * kernel_re
    conv = inverse(prod_re, prod_im, factor).reshape(lanes, length).T
    return (conv + skip_part[None, :] * product.astype(jnp.float32)).astype(jnp.bfloat16)


def local(
    gate_in, key_in, value_in, long_filter, gate_short, key_short, value_short, skip_gain, norm_gain
):
    tok, width = value_in.shape
    blocks = lax.axis_size("seq")
    narrow = width // blocks
    position = lax.axis_index("seq")
    skip_part = lax.dynamic_slice_in_dim(skip_gain, position * narrow, narrow, 0)
    prev_gate = passed_along(gate_in[tok - 2 :], "seq", 1)
    local_key, local_value, local_taps = (
        lax.all_to_all(key_in, "seq", split_axis=1, concat_axis=0, tiled=True),
        lax.all_to_all(value_in, "seq", split_axis=1, concat_axis=0, tiled=True),
        lax.all_to_all(long_filter, "seq", split_axis=1, concat_axis=0, tiled=True),
    )
    blank = jnp.zeros((2, narrow), jnp.bfloat16)
    key_part = lax.dynamic_slice_in_dim(key_short, position * narrow, narrow, 1)
    value_part = lax.dynamic_slice_in_dim(value_short, position * narrow, narrow, 1)
    local_product = (
        short_conv(local_key, blank, key_part) * short_conv(local_value, blank, value_part)
    ).astype(jnp.bfloat16)
    local_mixed = long_conv(local_product, local_taps, skip_part)
    mixed_in = lax.all_to_all(local_mixed, "seq", split_axis=0, concat_axis=1, tiled=True)
    gated = short_conv(gate_in, prev_gate, gate_short) * mixed_in.astype(jnp.float32)
    squares = jnp.sum(gated * gated, axis=1)
    total = lax.psum(squares, "ch")
    meansq = total / (width * lax.axis_size("ch"))
    return (gated * norm_gain[None, :] * lax.rsqrt(meansq + 1e-06)[:, None]).astype(jnp.bfloat16)


def solution(mesh):
    return jax.shard_map(
        local,
        mesh=mesh,
        in_specs=(
            P("seq", "ch"),
            P("seq", "ch"),
            P("seq", "ch"),
            P("seq", "ch"),
            P(None, "ch"),
            P(None, "ch"),
            P(None, "ch"),
            P("ch"),
            P("ch"),
        ),
        out_specs=P("seq", "ch"),
        check_vma=False,
    )
```

profile of v0, /device:TPU:8, one launch (start us, length us, event | category | flops | bytes accessed | tf_op | source)
XLA Modules:
  0.0 111.0 jit_solution(3934310177772360245)
XLA Ops:
  0.0 2.1 %copy.98 = bf16[256,1024]{0,1:T(8,128)(2,1)} copy(bf16[256,1024]{1,0:T(8,128)(2,1)} %param.10) | data formatting | bytes 1048576 | tf_op args[1]
  2.1 8.7 %all-to-all-start = ((bf16[256,32,32]{0,2,1:T(8,128)(2,1)}), bf16[256,32,32]{0,2,1:T(8,128)(2,1)S(1)}, u32[]{:S(2)}, u32[]{:S(2)}) async-start(bf16[256,32,32]{0,2,1:T(8,128)(2,1)} %bitcast.4), calls=%async_computation | async-start | bytes 1048576 | tf_op jit(solution)/shard_map/all_to_all | solution.py:109
  10.8 1.0 copy.100
  11.8 0.3 multiply_cosine_fusion
  12.1 0.3 multiply_sine_fusion.2
  12.3 8.1 %all-to-all-done = bf16[256,32,32]{0,2,1:T(8,128)(2,1)S(1)} async-done(((bf16[256,32,32]{0,2,1:T(8,128)(2,1)}), bf16[256,32,32]{0,2,1:T(8,128)(2,1)S(1)}, u32[]{:S(2)}, u32[]{:S(2)}) %all-to-all-start) | async-done | bytes 524320 | tf_op jit(solution)/shard_map/all_to_all | solution.py:109
  20.5 5.6 %all-to-all-start.1 = ((bf16[256,32,32]{0,2,1:T(8,128)(2,1)}), bf16[256,32,32]{0,2,1:T(8,128)(2,1)S(1)}, u32[]{:S(2)}, u32[]{:S(2)}) async-start(bf16[256,32,32]{0,2,1:T(8,128)(2,1)} %bitcast.9), calls=%async_computation.1 | async-start | bytes 1048576 | tf_op jit(solution)/shard_map/all_to_all | solution.py:110
  26.0 0.3 multiply_sine_fusion
  26.7 1.0 copy.106
  27.7 0.8 dynamic_slice.11
  28.5 0.3 multiply_cosine_fusion.3
  28.7 0.3 multiply_sine_fusion.3
  29.0 0.3 multiply_cosine_fusion.1
  29.3 0.3 multiply_sine_fusion.1
  29.5 6.2 %all-to-all-done.1 = bf16[256,32,32]{0,2,1:T(8,128)(2,1)S(1)} async-done(((bf16[256,32,32]{0,2,1:T(8,128)(2,1)}), bf16[256,32,32]{0,2,1:T(8,128)(2,1)S(1)}, u32[]{:S(2)}, u32[]{:S(2)}) %all-to-all-start.1) | async-done | bytes 524320 | tf_op jit(solution)/shard_map/all_to_all | solution.py:110
  35.7 5.7 %all-to-all-start.2 = ((bf16[256,32,32]{0,2,1:T(8,128)(2,1)}), bf16[256,32,32]{0,2,1:T(8,128)(2,1)S(1)}, u32[]{:S(2)}, u32[]{:S(2)}) async-start(bf16[256,32,32]{0,2,1:T(8,128)(2,1)} %bitcast.20), calls=%async_computation.2 | async-start | bytes 1048576 | tf_op jit(solution)/shard_map/all_to_all | solution.py:111
  41.5 0.8 constant_dynamic-slice_fusion
  42.4 8.6 %all-to-all-done.2 = bf16[256,32,32]{0,2,1:T(8,128)(2,1)S(1)} async-done(((bf16[256,32,32]{0,2,1:T(8,128)(2,1)}), bf16[256,32,32]{0,2,1:T(8,128)(2,1)S(1)}, u32[]{:S(2)}, u32[]{:S(2)}) %all-to-all-start.2) | async-done | bytes 524320 | tf_op jit(solution)/shard_map/all_to_all | solution.py:111
  51.2 0.4 pad_convert_fusion
  51.6 1.2 %fusion.34 = bf16[8192,32]{0,1:T(8,128)(2,1)S(1)} fusion(f32[8194,32]{0,1:T(8,128)S(1)} %get-tuple-element.20, f32[8194,32]{0,1:T(8,128)S(1)} %get-tuple-element.21, f32[32]{0:T(128)S(1)} %get-tuple-element.16, f32[32]{0:T(128)S(1)} %get-tuple-element.17, f32[32]{0:T(128)S(1)} %get-tuple-element.15, f32[32]{0:T(128)S(1)} %get-tuple-element.13, ...), kind=kLoop, calls=%fused_computation.40 | loop fusion | flops 3145728 | bytes 6816512 | tf_op jit(solution)/shard_map/convert_element_type | solution.py:118
  52.9 0.9 fusion.77
  53.9 0.9 fusion.75
  54.8 0.8 fusion.74
  55.6 0.8 fusion.76
  56.4 1.3 %fusion = f32[32,128,128]{2,1,0:T(8,128)S(1)} fusion(f32[128,32,128]{2,0,1:T(8,128)S(1)} %fusion.76, f32[128,32,128]{2,0,1:T(8,128)S(1)} %fusion.74, f32[128,128]{1,0:T(8,128)S(1)} %copy.109, f32[128,128]{1,0:T(8,128)S(1)} %copy.108), kind=kOutput, calls=%fused_computation | convolution fusion | flops 404455424 | bytes 6422528 | tf_op jit(solution)/shard_map/ckb,bm->ckm/dot_general | solution.py:59
  57.7 1.4 %fusion.2 = f32[32,128,128]{2,1,0:T(8,128)S(1)} fusion(f32[128,32,128]{2,0,1:T(8,128)S(1)} %fusion.76, f32[128,32,128]{2,0,1:T(8,128)S(1)} %fusion.74, f32[128,128]{1,0:T(8,128)S(1)} %copy.109, f32[128,128]{1,0:T(8,128)S(1)} %copy.108), kind=kOutput, calls=%fused_computation.2 | convolution fusion | flops 404455424 | bytes 6422528 | tf_op jit(solution)/shard_map/ckb,bm->ckm/dot_general | solution.py:56
  59.1 2.1 %fusion.47 = f32[32,128,128]{2,1,0:T(8,128)S(1)} fusion(f32[32,128,128]{2,1,0:T(8,128)S(1)} %fusion.77, f32[32,128,128]{2,1,0:T(8,128)S(1)} %fusion.75, f32[128,128]{0,1:T(8,128)S(1)} %get-tuple-element.22, f32[128,128]{0,1:T(8,128)S(1)} %get-tuple-element.23), kind=kOutput, calls=%fused_computation.62 | convolution fusion | flops 404455424 | bytes 6422528 | tf_op jit(solution)/shard_map/ckb,bm->ckm/dot_general | solution.py:59
  61.2 2.1 %fusion.49 = f32[32,128,128]{2,1,0:T(8,128)S(1)} fusion(f32[32,128,128]{2,1,0:T(8,128)S(1)} %fusion.77, f32[32,128,128]{2,1,0:T(8,128)S(1)} %fusion.75, f32[128,128]{0,1:T(8,128)S(1)} %get-tuple-element.22, f32[128,128]{0,1:T(8,128)S(1)} %get-tuple-element.23), kind=kOutput, calls=%fused_computation.63 | convolution fusion | flops 404455424 | bytes 6422528 | tf_op jit(solution)/shard_map/ckb,bm->ckm/dot_general | solution.py:56
  63.3 1.6 %fusion.21 = f32[32,128,128]{2,1,0:T(8,128)S(1)} fusion(f32[32,128,128]{2,1,0:T(8,128)S(1)} %fusion, f32[128,32,128]{2,0,1:T(8,128)S(1)} %fusion.76, f32[128,32,128]{2,0,1:T(8,128)S(1)} %fusion.74, f32[128,128]{1,0:T(8,128)S(1)} %copy.109, f32[128,128]{1,0:T(8,128)S(1)} %copy.108), kind=kOutput, calls=%fused_computation.27 | convolution fusion | flops 404979712 | bytes 8519680 | tf_op jit(solution)/shard_map/ckb,bm->ckm/dot_general | solution.py:59
  64.9 1.4 %fusion.18 = f32[32,128,128]{2,1,0:T(8,128)S(1)} fusion(f32[32,128,128]{2,1,0:T(8,128)S(1)} %fusion.2, f32[128,32,128]{2,0,1:T(8,128)S(1)} %fusion.76, f32[128,32,128]{2,0,1:T(8,128)S(1)} %fusion.74, f32[128,128]{1,0:T(8,128)S(1)} %copy.109, f32[128,128]{1,0:T(8,128)S(1)} %copy.108), kind=kOutput, calls=%fused_computation.26 | convolution fusion | flops 404979712 | bytes 8519680 | tf_op jit(solution)/shard_map/ckb,bm->ckm/dot_general | solution.py:56
  66.3 2.1 %convolution_subtract_fusion.1 = f32[32,128,128]{2,1,0:T(8,128)S(1)} fusion(f32[32,128,128]{2,1,0:T(8,128)S(1)} %fusion.49, f32[32,128,128]{2,1,0:T(8,128)S(1)} %fusion.77, f32[32,128,128]{2,1,0:T(8,128)S(1)} %fusion.75, f32[128,128]{0,1:T(8,128)S(1)} %get-tuple-element.22, f32[128,128]{0,1:T(8,128)S(1)} %get-tuple-element.23), kind=kOutput, calls=%fused_computation.31 | convolution fusion | flops 404979712 | bytes 8519680 | tf_op jit(solution)/shard_map/ckb,bm->ckm/dot_general | solution.py:56
  68.5 2.4 %multiply_add_fusion = (f32[32,128,128]{2,1,0:T(8,128)S(1)}, f32[32,128,128]{2,1,0:T(8,128)S(1)}) fusion(f32[32,128,128]{2,1,0:T(8,128)S(1)} %fusion.18, f32[32,128,128]{2,1,0:T(8,128)S(1)} %convolution_subtract_fusion.1, f32[32,128,128]{2,1,0:T(8,128)S(1)} %fusion.21, f32[32,128,128]{2,1,0:T(8,128)S(1)} %fusion.47, f32[32,128,128]{2,1,0:T(8,128)S(1)} %fusion.77, ...), kind=kOutput, calls=%fused_computation.22 | convolution fusion | flops 408125440 | bytes 16908288 | tf_op jit(solution)/shard_map/ckb,bm->ckm/dot_general | solution.py:59
  70.8 1.2 %fusion.53 = f32[32,128,128]{2,1,0:T(8,128)S(1)} fusion(f32[32,128,128]{2,1,0:T(8,128)S(1)} %get-tuple-element.8), kind=kOutput, calls=%fused_computation.76 | convolution fusion | flops 402882560 | bytes 4194304 | tf_op jit(solution)/shard_map/ckm,mn->ckn/dot_general | solution.py:71
  72.1 1.2 %fusion.57 = f32[32,128,128]{2,1,0:T(8,128)S(1)} fusion(f32[32,128,128]{2,1,0:T(8,128)S(1)} %get-tuple-element.8), kind=kOutput, calls=%fused_computation.80 | convolution fusion | flops 402882560 | bytes 4194304 | tf_op jit(solution)/shard_map/ckm,mn->ckn/dot_general | solution.py:68
  73.3 1.2 %convolution_add_fusion = f32[32,128,128]{2,1,0:T(8,128)S(1)} fusion(f32[32,128,128]{2,1,0:T(8,128)S(1)} %fusion.53, f32[32,128,128]{2,1,0:T(8,128)S(1)} %get-tuple-element.7), kind=kOutput, calls=%fused_computation.28 | convolution fusion | flops 403406848 | bytes 6291456 | tf_op jit(solution)/shard_map/ckm,mn->ckn/dot_general | solution.py:71
  74.6 1.2 %convolution_subtract_fusion = f32[32,128,128]{2,1,0:T(8,128)S(1)} fusion(f32[32,128,128]{2,1,0:T(8,128)S(1)} %fusion.57, f32[32,128,128]{2,1,0:T(8,128)S(1)} %get-tuple-element.7), kind=kOutput, calls=%fused_computation.29 | convolution fusion | flops 403406848 | bytes 6291456 | tf_op jit(solution)/shard_map/ckm,mn->ckn/dot_general | solution.py:68
  75.8 1.2 %fusion.10 = f32[32,128,64]{1,2,0:T(8,128)S(1)} fusion(f32[32,128,128]{2,1,0:T(8,128)S(1)} %convolution_add_fusion, f32[32,128,128]{2,1,0:T(8,128)S(1)} %convolution_subtract_fusion, f32[128,128]{1,0:T(8,128)S(1)} %copy.123, f32[128,128]{1,0:T(8,128)S(1)} %copy.120, f32[128,128]{0,1:T(8,128)S(1)} %multiply_sine_fusion.1), kind=kOutput, calls=%fused_computation.14 | convolution fusion | flops 202899456 | bytes 5439488 | tf_op jit(solution)/shard_map/pk,ckn->cpn/dot_general | solution.py:79
  77.0 1.0 fusion.27
  78.0 0.6 fusion.31
  78.7 0.9 copy.169
  79.5 5.6 %all-to-all-start.3 = ((bf16[32,256,32]{1,2,0:T(8,128)(2,1)}), bf16[32,256,32]{1,2,0:T(8,128)(2,1)S(1)}, u32[]{:S(2)}, u32[]{:S(2)}) async-start(bf16[32,256,32]{1,2,0:T(8,128)(2,1)} %bitcast.156), calls=%async_computation.3 | async-start | bytes 1048576 | tf_op jit(solution)/shard_map/all_to_all | solution.py:120
  85.3 2.1 %collective-permute-start = (bf16[2,1024]{0,1:T(8,128)(2,1)S(1)}, bf16[2,1024]{0,1:T(8,128)(2,1)S(1)}, u32[]{:S(2)}, u32[]{:S(2)}) collective-permute-start(bf16[2,1024]{0,1:T(8,128)(2,1)S(1)} %copy.96), channel_id=1, source_target_pairs={{0,4},{4,8},{8,12},{12,16},{16,20},{20,24},{24,28},{28,32},{32,36}... | collective-permute-start | bytes 12296 | tf_op jit(solution)/shard_map/ppermute | solution.py:17
  87.6 10.3 %collective-permute-done = bf16[2,1024]{0,1:T(8,128)(2,1)S(1)} collective-permute-done((bf16[2,1024]{0,1:T(8,128)(2,1)S(1)}, bf16[2,1024]{0,1:T(8,128)(2,1)S(1)}, u32[]{:S(2)}, u32[]{:S(2)}) %collective-permute-start) | collective-permute-done | bytes 4128 | tf_op jit(solution)/shard_map/ppermute | solution.py:17
  97.9 0.3 maximum_convert_fusion
  98.3 1.0 multiply_reduce_fusion
  99.3 10.5 %psum.7 = f32[256]{0:T(256)S(1)} all-reduce(f32[256]{0:T(256)S(1)} %get-tuple-element.5), channel_id=1, replica_groups=mesh['seq'=32,'ch'=4] {'ch'}, use_global_device_ids=true, to_apply=%region_1.2 | all-reduce | flops 256 | bytes 2048 | tf_op jit(solution)/shard_map/psum | solution.py:123
  109.8 0.2 multiply_convert_fusion
  110.0 1.0 copy.127
  (27 shorter events, 1.2 us)
Async XLA Ops:
  0.0 10.8 %copy-start.1 = (bf16[256,1024]{1,0:T(8,128)(2,1)S(1)}, bf16[256,1024]{1,0:T(8,128)(2,1)}, u32[]{:S(2)}) copy-start(bf16[256,1024]{1,0:T(8,128)(2,1)} %param.11) | copy-start | bytes 1572868
  2.1 24.6 %copy-start.2 = (bf16[256,1024]{1,0:T(8,128)(2,1)S(1)}, bf16[256,1024]{1,0:T(8,128)(2,1)}, u32[]{:S(2)}) copy-start(bf16[256,1024]{1,0:T(8,128)(2,1)} %param.12) | copy-start | bytes 1572868
  2.1 18.4 %all-to-all-start = ((bf16[256,32,32]{0,2,1:T(8,128)(2,1)}), bf16[256,32,32]{0,2,1:T(8,128)(2,1)S(1)}, u32[]{:S(2)}, u32[]{:S(2)}) async-start(bf16[256,32,32]{0,2,1:T(8,128)(2,1)} %bitcast.4), calls=%async_computation | async-start | bytes 1048576 | tf_op jit(solution)/shard_map/all_to_all | solution.py:109
  20.5 15.3 %all-to-all-start.1 = ((bf16[256,32,32]{0,2,1:T(8,128)(2,1)}), bf16[256,32,32]{0,2,1:T(8,128)(2,1)S(1)}, u32[]{:S(2)}, u32[]{:S(2)}) async-start(bf16[256,32,32]{0,2,1:T(8,128)(2,1)} %bitcast.9), calls=%async_computation.1 | async-start | bytes 1048576 | tf_op jit(solution)/shard_map/all_to_all | solution.py:110
  35.7 15.3 %all-to-all-start.2 = ((bf16[256,32,32]{0,2,1:T(8,128)(2,1)}), bf16[256,32,32]{0,2,1:T(8,128)(2,1)S(1)}, u32[]{:S(2)}, u32[]{:S(2)}) async-start(bf16[256,32,32]{0,2,1:T(8,128)(2,1)} %bitcast.20), calls=%async_computation.2 | async-start | bytes 1048576 | tf_op jit(solution)/shard_map/all_to_all | solution.py:111
  78.0 7.1 %copy-start = (bf16[256,1024]{1,0:T(8,128)(2,1)S(1)}, bf16[256,1024]{1,0:T(8,128)(2,1)}, u32[]{:S(2)}) copy-start(bf16[256,1024]{1,0:T(8,128)(2,1)} %param.9) | copy-start | bytes 1572868
  78.0 9.4 %copy-start.3 = (f32[3,1024]{1,0:T(4,128)S(1)}, f32[3,1024]{1,0:T(4,128)}, u32[]{:S(2)}) copy-start(f32[3,1024]{1,0:T(4,128)} %param.13) | copy-start | bytes 36868
  79.5 18.7 %all-to-all-start.3 = ((bf16[32,256,32]{1,2,0:T(8,128)(2,1)}), bf16[32,256,32]{1,2,0:T(8,128)(2,1)S(1)}, u32[]{:S(2)}, u32[]{:S(2)}) async-start(bf16[32,256,32]{1,2,0:T(8,128)(2,1)} %bitcast.156), calls=%async_computation.3 | async-start | bytes 1048576 | tf_op jit(solution)/shard_map/all_to_all | solution.py:120
  85.3 12.6 %collective-permute-start = (bf16[2,1024]{0,1:T(8,128)(2,1)S(1)}, bf16[2,1024]{0,1:T(8,128)(2,1)S(1)}, u32[]{:S(2)}, u32[]{:S(2)}) collective-permute-start(bf16[2,1024]{0,1:T(8,128)(2,1)S(1)} %copy.96), channel_id=1, source_target_pairs={{0,4},{4,8},{8,12},{12,16},{16,20},{20,24},{24,28},{28,32},{32,36}... | collective-permute-start | bytes 12296 | tf_op jit(solution)/shard_map/ppermute | solution.py:17
  98.2 11.5 %copy-start.4 = (f32[1024]{0:T(1024)S(1)}, f32[1024]{0:T(1024)}, u32[]{:S(2)}) copy-start(f32[1024]{0:T(1024)} %param.17) | copy-start | bytes 12292
where the time goes:
time: 112 us; the launch traced here: 111 us
  waiting for transfers between devices  33.3 us (30%)
  starting transfers between devices  27.6 us (25%)
  matrix products  24.9 us (22%)
  blocking collectives  10.5 us (9%)
  local copies, waits for them, and re-layouts  8.66 us (8%)
  other arithmetic  5.69 us (5%)
    psum x1, blocking collectives, local(): total = lax.psum(squares, 'ch')  10.5 us
    ppermute x1, waiting for transfers between devices, passed_along(): return lax.ppermute(array, axis, pairs)  10.3 us
    all_to_all x1, starting transfers between devices, local(): lax.all_to_all(key_in, 'seq', split_axis=1, concat_axis=0, tiled=True)  8.68 us
    all_to_all x1, waiting for transfers between devices, local(): lax.all_to_all(long_filter, 'seq', split_axis=1, concat_axis=0, tiled=True)  8.63 us
    all_to_all x1, waiting for transfers between devices, local(): lax.all_to_all(key_in, 'seq', split_axis=1, concat_axis=0, tiled=True)  8.14 us
    all_to_all x1, waiting for transfers between devices, local(): lax.all_to_all(value_in, 'seq', split_axis=1, concat_axis=0, tiled=True)  6.21 us
    all_to_all x1, starting transfers between devices, local(): lax.all_to_all(long_filter, 'seq', split_axis=1, concat_axis=0, tiled=True)  5.74 us
    all_to_all x1, starting transfers between devices, local(): lax.all_to_all(local_mixed, 'seq', split_axis=0, concat_axis=1, tiled=True)  5.56 us
  transfers between devices with their start and end apart: 5, of which 4 were waited for; matrix products, arithmetic and copies ran while one was open for 6% of the time, Pallas kernels for 0%

commit v1 on v0

v1 whole, which is shorter than its diff:
```python
import functools

import jax
import jax.numpy as jnp
from jax import lax
from jax.experimental import pallas as pl
from jax.experimental.pallas import tpu as pltpu
from jax.sharding import PartitionSpec as P

MESH = pl.DeviceIdType.MESH
F32, BF = jnp.float32, jnp.bfloat16
NT = (((1,), (1,)), ((), ()))

BLOCKS = 32
GROUPS = 4
TOK = 256
WIDTH = 1024
PARTS = 4
C = 8
SLOTS = 2
LANES = 128
SEGS = 64
ROWS = SEGS * C


def peer_at(me, step):
    y, z, core = me // 8, lax.rem(me // 2, 4), lax.rem(me, 2)
    return (
        lax.rem(y + step // 8, 4) * 8
        + lax.rem(z + lax.rem(step // 2, 4), 4) * 2
        + lax.rem(core + lax.rem(step, 2), 2)
    )


def exchange(me, ch, src, dst, part, send_sem, recv_sem):
    mine = pl.ds(pl.multiple_of(me * 16, 16), 16)
    pltpu.make_async_copy(src.at[part, mine], dst.at[part, mine], recv_sem.at[part]).start()

    def send(step, carry):
        peer = peer_at(me, step)
        pltpu.make_async_remote_copy(
            src_ref=src.at[part, pl.ds(pl.multiple_of(peer * 16, 16), 16)],
            dst_ref=dst.at[part, mine],
            send_sem=send_sem.at[part],
            recv_sem=recv_sem.at[part],
            device_id=(peer, ch),
            device_id_type=MESH,
        ).start()
        return carry

    lax.fori_loop(1, BLOCKS, send, 0)


def arrived(dst, part, recv_sem):
    pltpu.make_async_copy(dst.at[part], dst.at[part], recv_sem.at[part]).wait()


def sent(src, part, send_sem):
    piece = src.at[part, pl.ds(0, 16 * (BLOCKS - 1))]
    pltpu.make_async_copy(piece, piece, send_sem.at[part]).wait()


def lanes_of(block):
    return pl.ds(pl.multiple_of(block * LANES, LANES), LANES)


def short_conv(full, taps, block):
    at = lanes_of(block)
    return (
        taps[0:1, at] * full[8 : 8 + TOK, at]
        + taps[1:2, at] * full[7 : 7 + TOK, at]
        + taps[2:3, at] * full[6 : 6 + TOK, at]
    )


def split_rows(tokens, block, dst):
    first, second = tokens[:LANES].T, tokens[LANES:].T
    for group in range(LANES // C):
        rows = slice(C * group, C * group + C)
        pair = jnp.concatenate([first[rows], second[rows]], axis=0).astype(BF)
        owner = block * 4 + group // PARTS
        dst[group % PARTS, pl.ds(pl.multiple_of(owner * 16, 16), 16), :] = pair


def make_left(c, slot, taps, left):
    lane = lax.broadcasted_iota(jnp.int32, (8, LANES), 1)
    for u in range(8):
        here = taps[pl.ds((1 + 8 * u) * C + c, 8, stride=C), :]
        before = taps[pl.ds(8 * u * C + c, 8, stride=C), :]
        phases = []
        for r in range(4):
            by = 32 * (3 - r)
            if by:
                phases.append(pltpu.roll(jnp.where(lane >= LANES - by, before, here), by, 1))
            else:
                phases.append(here)
        left[slot, 32 + 32 * u : 64 + 32 * u, :] = jnp.concatenate(phases, axis=0).astype(BF)


def make_right(c, slot, flipped, right):
    lane = lax.broadcasted_iota(jnp.int32, (8, LANES), 1)
    row = lax.broadcasted_iota(jnp.int32, (8, LANES), 0)
    masks = [lane < 31 - 8 * o - row for o in range(4)]
    before = jnp.broadcast_to(flipped[pl.ds(c, 1), :], (8, LANES))
    for m in range(SEGS):
        b, g = m // 8, m % 8
        here = jnp.broadcast_to(flipped[pl.ds((m + 1) * C + c, 1), :], (8, LANES))
        phases = [
            pltpu.roll(
                jnp.where(masks[o], before, here), 97 + 8 * o, 1, stride=1, stride_axis=0
            )
            for o in range(4)
        ]
        half = LANES * (b % 2)
        right[slot, b // 2, 32 * g : 32 * g + 32, half : half + LANES] = jnp.concatenate(
            phases, axis=0
        ).astype(BF)
        before = here


def multiply(slot, left, right, sums):
    total = None
    for k in range(4):
        n = 256 - 64 * k
        lhs = jnp.concatenate([left[slot, 32 : 32 + n, :], left[slot, 0:n, :]], axis=1)
        part = lax.dot_general(lhs, right[slot, k], NT, preferred_element_type=F32)
        if total is None:
            total = [part[64 * i : 64 * i + 64] for i in range(4)]
        else:
            for i in range(k, 4):
                total[i] = total[i] + part[64 * (i - k) : 64 * (i - k) + 64]
    for u in range(8):
        for r in range(4):
            at = 32 * (u % 2) + 8 * r
            sums[slot, r, 8 + 8 * u : 16 + 8 * u, :] = total[u // 2][at : at + 8]


def fold(c, slot, skip, sums, plain, result):
    lane = lax.broadcasted_iota(jnp.int32, (8, LANES), 1)
    for u in range(8):
        y = None
        for d in range(4):
            v = None
            for j in range(4):
                r = (j + d) % 4
                low = sums[slot, r, 8 + 8 * u - j : 16 + 8 * u - j, 0:LANES]
                high = sums[slot, r, 4 + 8 * u - j : 12 + 8 * u - j, LANES : 2 * LANES]
                w = low + high
                v = w if v is None else jnp.where(lane >= 32 * j, w, v)
            if d:
                v = pltpu.roll(v, 32 * d, 1)
            y = v if y is None else y + v
        at = pl.ds(8 * u * C + c, 8, stride=C)
        result[at, :] = y + skip * plain[at, :]


def kernel(
    gate_hbm, key_hbm, value_hbm, filter_hbm,
    gate_short, key_short, value_short, skip_gain, norm_gain,
    out, scale,
    gate_in, key_in, value_in, filter_in, load_sem,
    gate_full, key_full, value_full,
    edge_out, edge_in, edge_send, edge_recv,
    filter_send, filter_recv, product_send, product_recv, mixed_send, mixed_recv,
    sems,
    gated, taps, plain, flipped, result, left, right, sums,
    square_send, square_recv, square_sems,
):
    me, ch = lax.axis_index("seq"), lax.axis_index("ch")
    loads = [
        pltpu.make_async_copy(src, dst, load_sem.at[i])
        for i, (src, dst) in enumerate(
            ((key_hbm, key_in), (value_hbm, value_in), (gate_hbm, gate_in), (filter_hbm, filter_in))
        )
    ]
    for load in loads:
        load.start()

    barrier = pltpu.get_barrier_semaphore()

    def greet(step, carry):
        pl.semaphore_signal(
            barrier, inc=1, device_id=(peer_at(me, step), ch), device_id_type=MESH
        )
        return carry

    lax.fori_loop(1, BLOCKS, greet, 0)
    for d in range(1, GROUPS):
        pl.semaphore_signal(
            barrier, inc=1, device_id=(me, lax.rem(ch + d, GROUPS)), device_id_type=MESH
        )

    for load in loads[:3]:
        load.wait()
    edge_out[...] = jnp.zeros_like(edge_out)
    for i, (src, full) in enumerate(
        ((key_in, key_full), (value_in, value_full), (gate_in, gate_full))
    ):
        full[8 : 8 + TOK, :] = src[...].astype(F32)
        edge_out[2 * i : 2 * i + 2, :] = full[6 + TOK : 8 + TOK, :]

    pl.semaphore_wait(barrier, BLOCKS - 1 + GROUPS - 1)
    edge = pltpu.make_async_remote_copy(
        src_ref=edge_out,
        dst_ref=edge_in,
        send_sem=edge_send,
        recv_sem=edge_recv,
        device_id=(lax.rem(me + 1, BLOCKS), ch),
        device_id_type=MESH,
    )
    edge.start()
    loads[3].wait()

    def cut_filter(block, carry):
        split_rows(filter_in[:, lanes_of(block)].astype(F32), block, filter_send)
        return carry

    lax.fori_loop(0, WIDTH // LANES, cut_filter, 0)
    filter_sems, product_sems, mixed_sems = (
        (sems.at[2 * i], sems.at[2 * i + 1]) for i in range(3)
    )
    exchange(me, ch, filter_send, filter_recv, 0, *filter_sems)

    edge.wait()
    for i, full in enumerate((key_full, value_full, gate_full)):
        full[6:8, :] = jnp.where(me == 0, 0.0, edge_in[2 * i : 2 * i + 2, :])

    def cut_product(block, carry):
        product = short_conv(key_full, key_short, block) * short_conv(
            value_full, value_short, block
        )
        split_rows(product.astype(BF).astype(F32), block, product_send)
        return carry

    lax.fori_loop(0, WIDTH // LANES, cut_product, 0)
    exchange(me, ch, product_send, product_recv, 0, *product_sems)

    def exchange_both(part, carry):
        exchange(me, ch, filter_send, filter_recv, part, *filter_sems)
        exchange(me, ch, product_send, product_recv, part, *product_sems)
        return carry

    lax.fori_loop(1, PARTS, exchange_both, 0)

    def turn_gate(block, carry):
        gate = short_conv(gate_full, gate_short, block)
        gated[lanes_of(block), 0:LANES] = gate[:LANES].T
        gated[lanes_of(block), LANES : 2 * LANES] = gate[LANES:].T
        return carry

    lax.fori_loop(0, WIDTH // LANES, turn_gate, 0)

    taps[0:C, :] = jnp.zeros((C, LANES), F32)
    flipped[0:C, :] = jnp.zeros((C, LANES), F32)
    for slot in range(SLOTS):
        left[slot, 0:32, :] = jnp.zeros((32, LANES), BF)
        for r in range(4):
            sums[slot, r, 0:8, :] = jnp.zeros((8, 2 * LANES), F32)
    rows = lax.broadcasted_iota(jnp.int32, (LANES, LANES), 0)
    cols = lax.broadcasted_iota(jnp.int32, (LANES, LANES), 1)
    flip = jnp.where(rows + cols == LANES - 1, 1.0, 0.0).astype(BF)

    def convolve(part, carry):
        arrived(filter_recv, part, filter_sems[1])
        taps[C:, :] = filter_recv[part].astype(F32)
        arrived(product_recv, part, product_sems[1])
        plain[...] = product_recv[part].astype(F32)
        flipped[C:, :] = jnp.dot(product_recv[part], flip, preferred_element_type=F32)

        def channels(i, carry):
            for slot in range(SLOTS):
                c = i * SLOTS + slot
                make_left(c, slot, taps, left)
                make_right(c, slot, flipped, right)
                multiply(slot, left, right, sums)
                skip = skip_gain[me * (PARTS * C) + part * C + c]
                fold(c, slot, skip, sums, plain, result)
            return carry

        lax.fori_loop(0, C // SLOTS, channels, 0)
        mixed_send[part] = result[...].astype(BF)
        exchange(me, ch, mixed_send, mixed_recv, part, *mixed_sems)
        return carry

    lax.fori_loop(0, PARTS, convolve, 0)

    def gate_part(part, squares):
        arrived(mixed_recv, part, mixed_sems[1])

        def gate_owner(owner, squares):
            pair = mixed_recv[part, pl.ds(pl.multiple_of(owner * 16, 16), 16), :].astype(F32)
            at = pl.ds(pl.multiple_of(owner * (PARTS * C) + part * C, C), C)
            g = gated[at, :] * jnp.concatenate([pair[:C], pair[C:]], axis=1)
            gated[at, :] = g
            return squares + g * g

        return lax.fori_loop(0, BLOCKS, gate_owner, squares, unroll=4)

    squares = lax.fori_loop(0, PARTS, gate_part, jnp.zeros((C, TOK), F32))
    square_send[...] = squares
    tells = [
        pltpu.make_async_remote_copy(
            src_ref=square_send,
            dst_ref=square_recv.at[d - 1],
            send_sem=square_sems.at[0, d - 1],
            recv_sem=square_sems.at[1, d - 1],
            device_id=(me, lax.rem(ch + d, GROUPS)),
            device_id_type=MESH,
        )
        for d in range(1, GROUPS)
    ]
    for tell in tells:
        tell.start()

    def turn_back(block, carry):
        at = lanes_of(block)
        out[:, at] = gated[at, :].T * norm_gain[0:1, at]
        return carry

    lax.fori_loop(0, WIDTH // LANES, turn_back, 0)
    for tell in tells:
        tell.wait()
    for d in range(GROUPS - 1):
        squares = squares + square_recv[d]
    meansq = jnp.sum(squares, axis=0, keepdims=True) / (WIDTH * GROUPS)
    inverse = lax.rsqrt(meansq + 1e-06)
    scale[...] = jnp.broadcast_to(inverse, (LANES, TOK)).T

    edge_free = [(filter_send, filter_sems), (product_send, product_sems), (mixed_send, mixed_sems)]
    for src, pair in edge_free:
        for part in range(PARTS):
            sent(src, part, pair[0])


def local(
    gate_in, key_in, value_in, long_filter, gate_short, key_short, value_short, skip_gain, norm_gain
):
    vmem = pl.BlockSpec(memory_space=pltpu.VMEM)
    smem = pl.BlockSpec(memory_space=pltpu.SMEM)
    hbm = pl.BlockSpec(memory_space=pl.ANY)
    parts = (PARTS, ROWS, LANES)
    gated, scale = pl.pallas_call(
        kernel,
        out_shape=(
            jax.ShapeDtypeStruct((TOK, WIDTH), F32),
            jax.ShapeDtypeStruct((TOK, LANES), F32),
        ),
        in_specs=[hbm] * 4 + [vmem] * 3 + [smem, vmem],
        out_specs=(vmem, vmem),
        scratch_shapes=[
            *[pltpu.VMEM((TOK, WIDTH), BF)] * 4,
            pltpu.SemaphoreType.DMA((4,)),
            *[pltpu.VMEM((8 + TOK, WIDTH), F32)] * 3,
            *[pltpu.VMEM((8, WIDTH), F32)] * 2,
            pltpu.SemaphoreType.DMA,
            pltpu.SemaphoreType.DMA,
            *[pltpu.VMEM(parts, BF)] * 6,
            pltpu.SemaphoreType.DMA((6, PARTS)),
            pltpu.VMEM((WIDTH, TOK), F32),
            pltpu.VMEM((ROWS + C, LANES), F32),
            pltpu.VMEM((ROWS, LANES), F32),
            pltpu.VMEM((ROWS + C, LANES), F32),
            pltpu.VMEM((ROWS, LANES), F32),
            pltpu.VMEM((SLOTS, 288, LANES), BF),
            pltpu.VMEM((SLOTS, 4, 256, 256), BF),
            pltpu.VMEM((SLOTS, 4, 72, 256), F32),
            pltpu.VMEM((C, TOK), F32),
            pltpu.VMEM((GROUPS - 1, C, TOK), F32),
            pltpu.SemaphoreType.DMA((2, GROUPS - 1)),
        ],
        compiler_params=pltpu.CompilerParams(
            collective_id=0, has_side_effects=True, vmem_limit_bytes=60 << 20
        ),
        name="hyena",
    )(
        gate_in, key_in, value_in, long_filter,
        gate_short, key_short, value_short, skip_gain, norm_gain.reshape(1, WIDTH),
    )
    return (gated * scale[:, :1]).astype(BF)


def solution(mesh):
    return jax.shard_map(
        local,
        mesh=mesh,
        in_specs=(
            P("seq", "ch"),
            P("seq", "ch"),
            P("seq", "ch"),
            P("seq", "ch"),
            P(None, "ch"),
            P(None, "ch"),
            P(None, "ch"),
            P("ch"),
            P("ch"),
        ),
        out_specs=P("seq", "ch"),
        check_vma=False,
    )
```

time: 112 us -> 49.7 us (0.44)
  the two profiles are of different devices: /device:TPU:8 before, /device:TPU:1 now
where the time goes in v1:
time: 49.7 us; the launch traced here: 49.4 us
  Pallas kernels  46.3 us (93%)
  other arithmetic  2.15 us (4%)
  local copies, waits for them, and re-layouts  1.01 us (2%)
    pallas_call x1, Pallas kernels, local(): pl.pallas_call(kernel, out_shape=(jax.ShapeDtypeStruct((TOK, WIDTH), F32)...  46.3 us
    convert_element_type x1, other arithmetic, local(): return (gated * scale[:, :1]).astype(BF)  2.15 us
    slice x1, local copies, waits for them, and re-layouts, local(): return (gated * scale[:, :1]).astype(BF)  1.01 us

profile of v1, /device:TPU:1, one launch (start us, length us, event | category | flops | bytes accessed | tf_op | source)
XLA Modules:
  0.0 49.4 jit_solution(3927849937826450733)
XLA Ops:
  0.0 46.3 %hyena.1 = (f32[256,1024]{1,0:T(8,128)}, f32[256,128]{1,0:T(8,128)}) custom-call(bf16[256,1024]{1,0:T(8,128)(2,1)} %gate_hbm.1, bf16[256,1024]{1,0:T(8,128)(2,1)} %key_hbm.1, bf16[256,1024]{1,0:T(8,128)(2,1)} %value_hbm.1, bf16[256,1024]{1,0:T(8,128)(2,1)} %filter_hbm.1, f32[3,1024]{1,0:T(4,128)} %gate_short.1, f32[3,1024]{1,0:T(4,128)} %key_short.1, ...), custom_call_target="tpu_custom_call" | custom-call | tf_op jit(solution)/shard_map/hyena/pallas_call | solution.py:342
  46.3 1.0 %slice_reduce_fusion = f32[256]{0:T(256)S(1)} fusion(f32[256,128]{1,0:T(8,128)} %get-tuple-element.8), kind=kLoop, calls=%fused_computation.1 | loop fusion | bytes 2048 | tf_op jit(solution)/shard_map/slice | solution.py:379
  47.3 2.1 %multiply_convert_fusion = bf16[256,1024]{1,0:T(8,128)(2,1)} fusion(f32[256,1024]{1,0:T(8,128)} %get-tuple-element.7, f32[256]{0:T(256)S(1)} %slice_reduce_fusion), kind=kLoop, calls=%fused_computation | loop fusion | flops 524288 | bytes 1573888 | tf_op jit(solution)/shard_map/convert_element_type | solution.py:379

commit v2 on v1

--- a/solution.py
+++ b/solution.py
@@ -23,21 +23,17 @@
 ROWS = SEGS * C
 
 
-def peer_at(me, step):
-    y, z, core = me // 8, lax.rem(me // 2, 4), lax.rem(me, 2)
-    return (
-        lax.rem(y + step // 8, 4) * 8
-        + lax.rem(z + lax.rem(step // 2, 4), 4) * 2
-        + lax.rem(core + lax.rem(step, 2), 2)
-    )
-
-
-def exchange(me, ch, src, dst, part, send_sem, recv_sem):
+def others(me):
+    ys = [lax.rem(me // 8 + d, 4) * 8 for d in range(4)]
+    zs = [lax.rem(me // 2 + d, 4) * 2 for d in range(4)]
+    cores = [lax.rem(me + d, 2) for d in range(2)]
+    return [y + z + core for y in ys for z in zs for core in cores][1:]
+
+
+def exchange(me, ch, peers, src, dst, part, send_sem, recv_sem):
     mine = pl.ds(pl.multiple_of(me * 16, 16), 16)
     pltpu.make_async_copy(src.at[part, mine], dst.at[part, mine], recv_sem.at[part]).start()
-
-    def send(step, carry):
-        peer = peer_at(me, step)
+    for peer in peers:
         pltpu.make_async_remote_copy(
             src_ref=src.at[part, pl.ds(pl.multiple_of(peer * 16, 16), 16)],
             dst_ref=dst.at[part, mine],
@@ -46,9 +42,6 @@
             device_id=(peer, ch),
             device_id_type=MESH,
         ).start()
-        return carry
-
-    lax.fori_loop(1, BLOCKS, send, 0)
 
 
 def arrived(dst, part, recv_sem):
@@ -157,47 +150,47 @@
 def kernel(
     gate_hbm, key_hbm, value_hbm, filter_hbm,
     gate_short, key_short, value_short, skip_gain, norm_gain,
-    out, scale,
+    out,
     gate_in, key_in, value_in, filter_in, load_sem,
     gate_full, key_full, value_full,
     edge_out, edge_in, edge_send, edge_recv,
     filter_send, filter_recv, product_send, product_recv, mixed_send, mixed_recv,
     sems,
     gated, taps, plain, flipped, result, left, right, sums,
-    square_send, square_recv, square_sems,
+    square_send, square_recv, square_sems, turned,
+    key_tail, value_tail, gate_tail, tail_sem,
 ):
     me, ch = lax.axis_index("seq"), lax.axis_index("ch")
+    tails = [
+        pltpu.make_async_copy(src.at[pl.ds(TOK - 16, 16)], dst, tail_sem.at[i])
+        for i, (src, dst) in enumerate(
+            ((key_hbm, key_tail), (value_hbm, value_tail), (gate_hbm, gate_tail))
+        )
+    ]
     loads = [
         pltpu.make_async_copy(src, dst, load_sem.at[i])
         for i, (src, dst) in enumerate(
-            ((key_hbm, key_in), (value_hbm, value_in), (gate_hbm, gate_in), (filter_hbm, filter_in))
+            ((filter_hbm, filter_in), (key_hbm, key_in), (value_hbm, value_in), (gate_hbm, gate_in))
         )
     ]
-    for load in loads:
+    for load in tails + loads:
         load.start()
 
     barrier = pltpu.get_barrier_semaphore()
 
-    def greet(step, carry):
-        pl.semaphore_signal(
-            barrier, inc=1, device_id=(peer_at(me, step), ch), device_id_type=MESH
-        )
-        return carry
-
-    lax.fori_loop(1, BLOCKS, greet, 0)
+    peers = others(me)
+    for peer in peers:
+        pl.semaphore_signal(barrier, inc=1, device_id=(peer, ch), device_id_type=MESH)
     for d in range(1, GROUPS):
         pl.semaphore_signal(
             barrier, inc=1, device_id=(me, lax.rem(ch + d, GROUPS)), device_id_type=MESH
         )
 
-    for load in loads[:3]:
+    for load in tails:
         load.wait()
     edge_out[...] = jnp.zeros_like(edge_out)
-    for i, (src, full) in enumerate(
-        ((key_in, key_full), (value_in, value_full), (gate_in, gate_full))
-    ):
-        full[8 : 8 + TOK, :] = src[...].astype(F32)
-        edge_out[2 * i : 2 * i + 2, :] = full[6 + TOK : 8 + TOK, :]
+    for i, tail in enumerate((key_tail, value_tail, gate_tail)):
+        edge_out[2 * i : 2 * i + 2, :] = tail[...].astype(F32)[14:16]
 
     pl.semaphore_wait(barrier, BLOCKS - 1 + GROUPS - 1)
     edge = pltpu.make_async_remote_copy(
@@ -209,7 +202,7 @@
         device_id_type=MESH,
     )
     edge.start()
-    loads[3].wait()
+    loads[0].wait()
 
     def cut_filter(block, carry):
         split_rows(filter_in[:, lanes_of(block)].astype(F32), block, filter_send)
@@ -219,8 +212,13 @@
     filter_sems, product_sems, mixed_sems = (
         (sems.at[2 * i], sems.at[2 * i + 1]) for i in range(3)
     )
-    exchange(me, ch, filter_send, filter_recv, 0, *filter_sems)
-
+    exchange(me, ch, peers, filter_send, filter_recv, 0, *filter_sems)
+
+    for load, src, full in zip(
+        loads[1:], (key_in, value_in, gate_in), (key_full, value_full, gate_full)
+    ):
+        load.wait()
+        full[8 : 8 + TOK, :] = src[...].astype(F32)
     edge.wait()
     for i, full in enumerate((key_full, value_full, gate_full)):
         full[6:8, :] = jnp.where(me == 0, 0.0, edge_in[2 * i : 2 * i + 2, :])
@@ -233,11 +231,11 @@
         return carry
 
     lax.fori_loop(0, WIDTH // LANES, cut_product, 0)
-    exchange(me, ch, product_send, product_recv, 0, *product_sems)
+    exchange(me, ch, peers, product_send, product_recv, 0, *product_sems)
 
     def exchange_both(part, carry):
-        exchange(me, ch, filter_send, filter_recv, part, *filter_sems)
-        exchange(me, ch, product_send, product_recv, part, *product_sems)
+        exchange(me, ch, peers, filter_send, filter_recv, part, *filter_sems)
+        exchange(me, ch, peers, product_send, product_recv, part, *product_sems)
         return carry
 
     lax.fori_loop(1, PARTS, exchange_both, 0)
@@ -279,7 +277,7 @@
 
         lax.fori_loop(0, C // SLOTS, channels, 0)
         mixed_send[part] = result[...].astype(BF)
-        exchange(me, ch, mixed_send, mixed_recv, part, *mixed_sems)
+        exchange(me, ch, peers, mixed_send, mixed_recv, part, *mixed_sems)
         return carry
 
     lax.fori_loop(0, PARTS, convolve, 0)
@@ -314,7 +312,7 @@
 
     def turn_back(block, carry):
         at = lanes_of(block)
-        out[:, at] = gated[at, :].T * norm_gain[0:1, at]
+        turned[:, at] = gated[at, :].T * norm_gain[0:1, at]
         return carry
 
     lax.fori_loop(0, WIDTH // LANES, turn_back, 0)
@@ -324,7 +322,11 @@
         squares = squares + square_recv[d]
     meansq = jnp.sum(squares, axis=0, keepdims=True) / (WIDTH * GROUPS)
     inverse = lax.rsqrt(meansq + 1e-06)
-    scale[...] = jnp.broadcast_to(inverse, (LANES, TOK)).T
+    scale = jnp.broadcast_to(inverse, (LANES, TOK)).T
+
+    for block in range(WIDTH // LANES):
+        at = slice(LANES * block, LANES * block + LANES)
+        out[:, at] = (turned[:, at] * scale).astype(BF)
 
     edge_free = [(filter_send, filter_sems), (product_send, product_sems), (mixed_send, mixed_sems)]
     for src, pair in edge_free:
@@ -339,14 +341,11 @@
     smem = pl.BlockSpec(memory_space=pltpu.SMEM)
     hbm = pl.BlockSpec(memory_space=pl.ANY)
     parts = (PARTS, ROWS, LANES)
-    gated, scale = pl.pallas_call(
+    return pl.pallas_call(
         kernel,
-        out_shape=(
-            jax.ShapeDtypeStruct((TOK, WIDTH), F32),
-            jax.ShapeDtypeStruct((TOK, LANES), F32),
-        ),
+        out_shape=jax.ShapeDtypeStruct((TOK, WIDTH), BF),
         in_specs=[hbm] * 4 + [vmem] * 3 + [smem, vmem],
-        out_specs=(vmem, vmem),
+        out_specs=vmem,
         scratch_shapes=[
             *[pltpu.VMEM((TOK, WIDTH), BF)] * 4,
             pltpu.SemaphoreType.DMA((4,)),
@@ -367,6 +366,9 @@
             pltpu.VMEM((C, TOK), F32),
             pltpu.VMEM((GROUPS - 1, C, TOK), F32),
             pltpu.SemaphoreType.DMA((2, GROUPS - 1)),
+            pltpu.VMEM((TOK, WIDTH), F32),
+            *[pltpu.VMEM((16, WIDTH), BF)] * 3,
+            pltpu.SemaphoreType.DMA((3,)),
         ],
         compiler_params=pltpu.CompilerParams(
             collective_id=0, has_side_effects=True, vmem_limit_bytes=60 << 20
@@ -376,7 +378,6 @@
         gate_in, key_in, value_in, long_filter,
         gate_short, key_short, value_short, skip_gain, norm_gain.reshape(1, WIDTH),
     )
-    return (gated * scale[:, :1]).astype(BF)
 
 
 def solution(mesh):

time: 49.7 us -> 45.1 us (0.907)
  Pallas kernels: 46.3 us -> 43 us
  other arithmetic: 2.15 us -> 0 us
  local copies, waits for them, and re-layouts: 1.01 us -> 1.87 us
    pallas_call x1, Pallas kernels: 46.3 us -> 43 us  [local(): pl.pallas_call(kernel, out_shape=jax.ShapeDtypeStruct((TOK, WIDTH), BF),...]
    convert_element_type x1 -> x0, other arithmetic: 2.15 us -> none  [local(): return (gated * scale[:, :1]).astype(BF)]
    unnamed x0 -> x1, local copies, waits for them, and re-layouts: none -> 1.87 us
    slice x1 -> x0, local copies, waits for them, and re-layouts: 1.01 us -> none  [local(): return (gated * scale[:, :1]).astype(BF)]
where the time goes in v2:
time: 45.1 us; the launch traced here: 44.9 us
  Pallas kernels  43 us (95%)
  local copies, waits for them, and re-layouts  1.87 us (4%)
    pallas_call x1, Pallas kernels, local(): pl.pallas_call(kernel, out_shape=jax.ShapeDtypeStruct((TOK, WIDTH), BF),...  43 us
    unnamed x1, local copies, waits for them, and re-layouts  1.87 us

profile of v2, /device:TPU:1, one launch (start us, length us, event | category | flops | bytes accessed | tf_op | source)
XLA Modules:
  0.0 44.9 jit_solution(622458785294898528)
XLA Ops:
  0.0 43.0 %hyena.1 = bf16[256,1024]{1,0:T(8,128)(2,1)} custom-call(bf16[256,1024]{1,0:T(8,128)(2,1)} %gate_hbm.1, bf16[256,1024]{1,0:T(8,128)(2,1)} %key_hbm.1, bf16[256,1024]{1,0:T(8,128)(2,1)} %value_hbm.1, bf16[256,1024]{1,0:T(8,128)(2,1)} %filter_hbm.1, f32[3,1024]{1,0:T(4,128)} %gate_short.1, f32[3,1024]{1,0:T(4,128)} %key_short.1, f32[3,1024]{1,0:T(4,128)} %value_short.1, ...), custom_call_target="tpu_custom_call" | custom-call | tf_op jit(solution)/shard_map/hyena/pallas_call | solution.py:344
  43.0 1.9 %copy.11 = bf16[256,1024]{1,0:T(8,128)(2,1)} copy(bf16[256,1024]{1,0:T(8,128)(2,1)} %hyena.1) | data formatting | bytes 1048576

commit v3 on v2

--- a/solution.py
+++ b/solution.py
@@ -17,8 +17,9 @@
 WIDTH = 1024
 PARTS = 4
 C = 8
-SLOTS = 2
+SLOTS = 4
 LANES = 128
+STAGES = (2, 1, 0)
 SEGS = 64
 ROWS = SEGS * C
 
@@ -88,6 +89,8 @@
             else:
                 phases.append(here)
         left[slot, 32 + 32 * u : 64 + 32 * u, :] = jnp.concatenate(phases, axis=0).astype(BF)
+        if u % 2:
+            yield
 
 
 def make_right(c, slot, flipped, right):
@@ -109,6 +112,8 @@
             phases, axis=0
         ).astype(BF)
         before = here
+        if m % 16 == 15:
+            yield
 
 
 def multiply(slot, left, right, sums):
@@ -122,10 +127,20 @@
         else:
             for i in range(k, 4):
                 total[i] = total[i] + part[64 * (i - k) : 64 * (i - k) + 64]
+        if k < 3:
+            yield
     for u in range(8):
         for r in range(4):
             at = 32 * (u % 2) + 8 * r
-            sums[slot, r, 8 + 8 * u : 16 + 8 * u, :] = total[u // 2][at : at + 8]
+            sums[slot, r, 12 + 8 * u : 20 + 8 * u, LANES:] = total[u // 2][at : at + 8, LANES:]
+    for u in range(8):
+        for r in range(4):
+            at = 32 * (u % 2) + 8 * r
+            rows = slice(8 + 8 * u, 16 + 8 * u)
+            sums[slot, r, rows, 0:LANES] = (
+                total[u // 2][at : at + 8, 0:LANES] + sums[slot, r, rows, LANES:]
+            )
+    yield
 
 
 def fold(c, slot, skip, sums, plain, result):
@@ -136,15 +151,15 @@
             v = None
             for j in range(4):
                 r = (j + d) % 4
-                low = sums[slot, r, 8 + 8 * u - j : 16 + 8 * u - j, 0:LANES]
-                high = sums[slot, r, 4 + 8 * u - j : 12 + 8 * u - j, LANES : 2 * LANES]
-                w = low + high
+                w = sums[slot, r, 8 + 8 * u - j : 16 + 8 * u - j, 0:LANES]
                 v = w if v is None else jnp.where(lane >= 32 * j, w, v)
             if d:
                 v = pltpu.roll(v, 32 * d, 1)
             y = v if y is None else y + v
         at = pl.ds(8 * u * C + c, 8, stride=C)
         result[at, :] = y + skip * plain[at, :]
+        if u % 2:
+            yield
 
 
 def kernel(
@@ -238,7 +253,6 @@
         exchange(me, ch, peers, product_send, product_recv, part, *product_sems)
         return carry
 
-    lax.fori_loop(1, PARTS, exchange_both, 0)
 
     def turn_gate(block, carry):
         gate = short_conv(gate_full, gate_short, block)
@@ -247,13 +261,14 @@
         return carry
 
     lax.fori_loop(0, WIDTH // LANES, turn_gate, 0)
+    lax.fori_loop(1, PARTS, exchange_both, 0)
 
     taps[0:C, :] = jnp.zeros((C, LANES), F32)
     flipped[0:C, :] = jnp.zeros((C, LANES), F32)
     for slot in range(SLOTS):
         left[slot, 0:32, :] = jnp.zeros((32, LANES), BF)
         for r in range(4):
-            sums[slot, r, 0:8, :] = jnp.zeros((8, 2 * LANES), F32)
+            sums[slot, r, 0:16, :] = jnp.zeros((16, 2 * LANES), F32)
     rows = lax.broadcasted_iota(jnp.int32, (LANES, LANES), 0)
     cols = lax.broadcasted_iota(jnp.int32, (LANES, LANES), 1)
     flip = jnp.where(rows + cols == LANES - 1, 1.0, 0.0).astype(BF)
@@ -266,13 +281,27 @@
         flipped[C:, :] = jnp.dot(product_recv[part], flip, preferred_element_type=F32)
 
         def channels(i, carry):
+            work = []
             for slot in range(SLOTS):
                 c = i * SLOTS + slot
-                make_left(c, slot, taps, left)
-                make_right(c, slot, flipped, right)
-                multiply(slot, left, right, sums)
                 skip = skip_gain[me * (PARTS * C) + part * C + c]
-                fold(c, slot, skip, sums, plain, result)
+                work.append(
+                    (
+                        (make_left(c, slot, taps, left), make_right(c, slot, flipped, right)),
+                        (multiply(slot, left, right, sums),),
+                        (fold(c, slot, skip, sums, plain, result),),
+                    )
+                )
+            for beat in range(SLOTS + 2):
+                turns = [
+                    steps
+                    for stage in STAGES
+                    if 0 <= beat - stage < SLOTS
+                    for steps in work[beat - stage][stage]
+                ]
+                for _ in range(4):
+                    for steps in turns:
+                        next(steps, None)
             return carry
 
         lax.fori_loop(0, C // SLOTS, channels, 0)
@@ -362,7 +391,7 @@
             pltpu.VMEM((ROWS, LANES), F32),
             pltpu.VMEM((SLOTS, 288, LANES), BF),
             pltpu.VMEM((SLOTS, 4, 256, 256), BF),
-            pltpu.VMEM((SLOTS, 4, 72, 256), F32),
+            pltpu.VMEM((SLOTS, 4, 80, 256), F32),
             pltpu.VMEM((C, TOK), F32),
             pltpu.VMEM((GROUPS - 1, C, TOK), F32),
             pltpu.SemaphoreType.DMA((2, GROUPS - 1)),

time: 45.1 us -> 42.1 us (0.933)
  Pallas kernels: 43 us -> 40 us
    pallas_call x1, Pallas kernels: 43 us -> 40 us  [local(): pl.pallas_call(kernel, out_shape=jax.ShapeDtypeStruct((TOK, WIDTH), BF),...]
where the time goes in v3:
time: 42.1 us; the launch traced here: 41.8 us
  Pallas kernels  40 us (95%)
  local copies, waits for them, and re-layouts  1.87 us (4%)
    pallas_call x1, Pallas kernels, local(): pl.pallas_call(kernel, out_shape=jax.ShapeDtypeStruct((TOK, WIDTH), BF),...  40 us
    unnamed x1, local copies, waits for them, and re-layouts  1.87 us

profile of v3, /device:TPU:1, one launch (start us, length us, event | category | flops | bytes accessed | tf_op | source)
XLA Modules:
  0.0 41.8 jit_solution(6482284626247339297)
XLA Ops:
  0.0 40.0 %hyena.1 = bf16[256,1024]{1,0:T(8,128)(2,1)} custom-call(bf16[256,1024]{1,0:T(8,128)(2,1)} %gate_hbm.1, bf16[256,1024]{1,0:T(8,128)(2,1)} %key_hbm.1, bf16[256,1024]{1,0:T(8,128)(2,1)} %value_hbm.1, bf16[256,1024]{1,0:T(8,128)(2,1)} %filter_hbm.1, f32[3,1024]{1,0:T(4,128)} %gate_short.1, f32[3,1024]{1,0:T(4,128)} %key_short.1, f32[3,1024]{1,0:T(4,128)} %value_short.1, ...), custom_call_target="tpu_custom_call" | custom-call | tf_op jit(solution)/shard_map/hyena/pallas_call | solution.py:373
  40.0 1.9 %copy.11 = bf16[256,1024]{1,0:T(8,128)(2,1)} copy(bf16[256,1024]{1,0:T(8,128)(2,1)} %hyena.1) | data formatting | bytes 1048576

commit v4 on v3

--- a/solution.py
+++ b/solution.py
@@ -72,8 +72,8 @@
     for group in range(LANES // C):
         rows = slice(C * group, C * group + C)
         pair = jnp.concatenate([first[rows], second[rows]], axis=0).astype(BF)
-        owner = block * 4 + group // PARTS
-        dst[group % PARTS, pl.ds(pl.multiple_of(owner * 16, 16), 16), :] = pair
+        owner = lax.rem(block, 2) * (LANES // C) + group
+        dst[block // 2, pl.ds(pl.multiple_of(owner * 16, 16), 16), :] = pair
 
 
 def make_left(c, slot, taps, left):
@@ -223,44 +223,46 @@
         split_rows(filter_in[:, lanes_of(block)].astype(F32), block, filter_send)
         return carry
 
-    lax.fori_loop(0, WIDTH // LANES, cut_filter, 0)
     filter_sems, product_sems, mixed_sems = (
         (sems.at[2 * i], sems.at[2 * i + 1]) for i in range(3)
     )
+    lax.fori_loop(0, 2, cut_filter, 0)
     exchange(me, ch, peers, filter_send, filter_recv, 0, *filter_sems)
 
-    for load, src, full in zip(
-        loads[1:], (key_in, value_in, gate_in), (key_full, value_full, gate_full)
-    ):
+    for load in loads[1:]:
         load.wait()
-        full[8 : 8 + TOK, :] = src[...].astype(F32)
     edge.wait()
     for i, full in enumerate((key_full, value_full, gate_full)):
         full[6:8, :] = jnp.where(me == 0, 0.0, edge_in[2 * i : 2 * i + 2, :])
 
     def cut_product(block, carry):
+        at = lanes_of(block)
+        key_full[8 : 8 + TOK, at] = key_in[:, at].astype(F32)
+        value_full[8 : 8 + TOK, at] = value_in[:, at].astype(F32)
         product = short_conv(key_full, key_short, block) * short_conv(
             value_full, value_short, block
         )
         split_rows(product.astype(BF).astype(F32), block, product_send)
         return carry
 
-    lax.fori_loop(0, WIDTH // LANES, cut_product, 0)
+    lax.fori_loop(0, 2, cut_product, 0)
     exchange(me, ch, peers, product_send, product_recv, 0, *product_sems)
 
     def exchange_both(part, carry):
+        lax.fori_loop(2 * part, 2 * part + 2, cut_filter, 0)
         exchange(me, ch, peers, filter_send, filter_recv, part, *filter_sems)
+        lax.fori_loop(2 * part, 2 * part + 2, cut_product, 0)
         exchange(me, ch, peers, product_send, product_recv, part, *product_sems)
         return carry
 
-
     def turn_gate(block, carry):
+        at = lanes_of(block)
+        gate_full[8 : 8 + TOK, at] = gate_in[:, at].astype(F32)
         gate = short_conv(gate_full, gate_short, block)
         gated[lanes_of(block), 0:LANES] = gate[:LANES].T
         gated[lanes_of(block), LANES : 2 * LANES] = gate[LANES:].T
         return carry
 
-    lax.fori_loop(0, WIDTH // LANES, turn_gate, 0)
     lax.fori_loop(1, PARTS, exchange_both, 0)
 
     taps[0:C, :] = jnp.zeros((C, LANES), F32)
@@ -284,7 +286,7 @@
             work = []
             for slot in range(SLOTS):
                 c = i * SLOTS + slot
-                skip = skip_gain[me * (PARTS * C) + part * C + c]
+                skip = skip_gain[part * (BLOCKS * C) + me * C + c]
                 work.append(
                     (
                         (make_left(c, slot, taps, left), make_right(c, slot, flipped, right)),
@@ -310,13 +312,14 @@
         return carry
 
     lax.fori_loop(0, PARTS, convolve, 0)
+    lax.fori_loop(0, WIDTH // LANES, turn_gate, 0)
 
     def gate_part(part, squares):
         arrived(mixed_recv, part, mixed_sems[1])
 
         def gate_owner(owner, squares):
             pair = mixed_recv[part, pl.ds(pl.multiple_of(owner * 16, 16), 16), :].astype(F32)
-            at = pl.ds(pl.multiple_of(owner * (PARTS * C) + part * C, C), C)
+            at = pl.ds(pl.multiple_of(part * (BLOCKS * C) + owner * C, C), C)
             g = gated[at, :] * jnp.concatenate([pair[:C], pair[C:]], axis=1)
             gated[at, :] = g
             return squares + g * g

time: 42.1 us -> 41.2 us (0.979)
  Pallas kernels: 40 us -> 39.1 us
    pallas_call x1, Pallas kernels: 40 us -> 39.1 us  [local(): pl.pallas_call(kernel, out_shape=jax.ShapeDtypeStruct((TOK, WIDTH), BF),...]
where the time goes in v4:
time: 41.2 us; the launch traced here: 41 us
  Pallas kernels  39.1 us (95%)
  local copies, waits for them, and re-layouts  1.87 us (5%)
    pallas_call x1, Pallas kernels, local(): pl.pallas_call(kernel, out_shape=jax.ShapeDtypeStruct((TOK, WIDTH), BF),...  39.1 us
    unnamed x1, local copies, waits for them, and re-layouts  1.87 us

profile of v4, /device:TPU:1, one launch (start us, length us, event | category | flops | bytes accessed | tf_op | source)
XLA Modules:
  0.0 41.0 jit_solution(2328923519842134999)
XLA Ops:
  0.0 39.1 %hyena.1 = bf16[256,1024]{1,0:T(8,128)(2,1)} custom-call(bf16[256,1024]{1,0:T(8,128)(2,1)} %gate_hbm.1, bf16[256,1024]{1,0:T(8,128)(2,1)} %key_hbm.1, bf16[256,1024]{1,0:T(8,128)(2,1)} %value_hbm.1, bf16[256,1024]{1,0:T(8,128)(2,1)} %filter_hbm.1, f32[3,1024]{1,0:T(4,128)} %gate_short.1, f32[3,1024]{1,0:T(4,128)} %key_short.1, f32[3,1024]{1,0:T(4,128)} %value_short.1, ...), custom_call_target="tpu_custom_call" | custom-call | tf_op jit(solution)/shard_map/hyena/pallas_call | solution.py:376
  39.1 1.9 %copy.11 = bf16[256,1024]{1,0:T(8,128)(2,1)} copy(bf16[256,1024]{1,0:T(8,128)(2,1)} %hyena.1) | data formatting | bytes 1048576

commit v5 on v4

--- a/solution.py
+++ b/solution.py
@@ -28,7 +28,12 @@
     ys = [lax.rem(me // 8 + d, 4) * 8 for d in range(4)]
     zs = [lax.rem(me // 2 + d, 4) * 2 for d in range(4)]
     cores = [lax.rem(me + d, 2) for d in range(2)]
-    return [y + z + core for y in ys for z in zs for core in cores][1:]
+    near = (0, 1, 2, 1)
+    order = sorted(
+        ((dy, dz, dc) for dy in range(4) for dz in range(4) for dc in range(2)),
+        key=lambda d: -near[d[0]] - near[d[1]],
+    )
+    return [ys[dy] + zs[dz] + cores[dc] for dy, dz, dc in order if dy + dz + dc]
 
 
 def exchange(me, ch, peers, src, dst, part, send_sem, recv_sem):

time: 41.2 us -> 40.4 us (0.981)
  Pallas kernels: 39.1 us -> 38.3 us
    pallas_call x1, Pallas kernels: 39.1 us -> 38.3 us  [local(): pl.pallas_call(kernel, out_shape=jax.ShapeDtypeStruct((TOK, WIDTH), BF),...]
where the time goes in v5:
time: 40.4 us; the launch traced here: 40.1 us
  Pallas kernels  38.3 us (95%)
  local copies, waits for them, and re-layouts  1.87 us (5%)
    pallas_call x1, Pallas kernels, local(): pl.pallas_call(kernel, out_shape=jax.ShapeDtypeStruct((TOK, WIDTH), BF),...  38.3 us
    unnamed x1, local copies, waits for them, and re-layouts  1.87 us

profile of v5, /device:TPU:1, one launch (start us, length us, event | category | flops | bytes accessed | tf_op | source)
XLA Modules:
  0.0 40.1 jit_solution(5426924099184581089)
XLA Ops:
  0.0 38.3 %hyena.1 = bf16[256,1024]{1,0:T(8,128)(2,1)} custom-call(bf16[256,1024]{1,0:T(8,128)(2,1)} %gate_hbm.1, bf16[256,1024]{1,0:T(8,128)(2,1)} %key_hbm.1, bf16[256,1024]{1,0:T(8,128)(2,1)} %value_hbm.1, bf16[256,1024]{1,0:T(8,128)(2,1)} %filter_hbm.1, f32[3,1024]{1,0:T(4,128)} %gate_short.1, f32[3,1024]{1,0:T(4,128)} %key_short.1, f32[3,1024]{1,0:T(4,128)} %value_short.1, ...), custom_call_target="tpu_custom_call" | custom-call | tf_op jit(solution)/shard_map/hyena/pallas_call | solution.py:381
  38.3 1.9 %copy.11 = bf16[256,1024]{1,0:T(8,128)(2,1)} copy(bf16[256,1024]{1,0:T(8,128)(2,1)} %hyena.1) | data formatting | bytes 1048576
